TPU v7x, 32 devices: a whole 2x2x4 slice. The times are simulated.
32 devices in a mesh: seq: 4 (over z), dom: 8 (over y, x, core).
Axes of the slice: x: 2, y: 2, z: 4, core: 2. Of those that a mesh axis runs over, the one named last changes fastest.
Arguments:
- nodes: bfloat16 [8, 1536, 1024], P('dom', 'seq'), may hold values from -6 to 6
- norm_gain: float32 [1024], replicated, may hold values from 0.1 to 1.9
- input_proj: bfloat16 [1024, 3, 1024], replicated, may hold values from -0.1875 to 0.1875
- output_proj: bfloat16 [1024, 1024], replicated, may hold values from -0.1875 to 0.1875
- final_gain: float32 [1024], replicated, may hold values from 0.1 to 1.9
- block_list: int32 [96, 12], replicated, may hold values from -1 to 95, as said below
- block_count: int32 [96], replicated, may hold values from 8 to 12
Outputs:
- layer_out: bfloat16 [8, 1536, 1024], P('dom', 'seq')
Inputs may be any that keep to these rules, and one draw needn't show every extreme that they name: `block_list`: entries 0 to block_count - 1 of a query block's list are live, the others are -1. Entry 0 is the query block itself, entries 1 to 3 are other blocks of its partition (1536 consecutive nodes), later live entries lie in other partitions, and no block appears twice in one list. Over all query blocks of one partition at most 2 distinct blocks of any one other partition are listed, and in every draw each partition lists exactly 2 blocks from some other partition.
All inputs are finite; a program needn't handle non-finite values.
Results may differ from a plain program's by a relative error of at most 0.014.
The roundings to bfloat16 on the way count: a program that leaves them out, or rounds other values in their place, can miss the bound.
Values may be sent and summed in bfloat16 or wider, within the bound.
A program may use at most 128 MiB of HBM per device.

v0:
```python
import functools

import jax
import jax.numpy as jnp
from jax import lax
from jax.experimental import pallas as pl
from jax.experimental.pallas import tpu as pltpu
from jax.sharding import PartitionSpec as P

HD = 64
BLK = 128
KMAX = 12
CAP = 2
GW = 256
GH = GW // HD
CHUNKS = 4
MESH = pl.DeviceIdType.MESH


def dot(a, b, dims=((1,), (0,))):
    return lax.dot_general(a, b, (dims, ((), ())), preferred_element_type=jnp.float32)


def gather_kernel(seq_size, dom_size, pick_ref, nodes_ref, gain_ref, *refs):
    local = refs[:CHUNKS]
    remote = refs[CHUNKS]
    stage, zsend, zrecv, dsend, drecv = refs[CHUNKS + 1 :]
    rows, width = nodes_ref.shape
    cw = width // CHUNKS
    z = lax.axis_index("seq")
    me = lax.axis_index("dom")
    last = seq_size - 1

    barrier = pltpu.get_barrier_semaphore()

    @pl.when(z > 0)
    def _():
        pl.semaphore_signal(barrier, inc=1, device_id=(z - 1, me), device_id_type=MESH)

    @pl.when(z < last)
    def _():
        pl.semaphore_signal(barrier, inc=1, device_id=(z + 1, me), device_id_type=MESH)

    for o in range(1, dom_size):
        pl.semaphore_signal(
            barrier, inc=1, device_id=(z, lax.rem(me + o, dom_size)), device_id_type=MESH
        )

    step = BLK
    held = rows // BLK
    for r in range(0, rows, step):
        wide = nodes_ref[r : r + step, :].astype(jnp.float32)
        center = jnp.mean(wide, axis=-1, keepdims=True)
        moved = wide - center
        spread = jnp.mean(jnp.square(moved), axis=-1, keepdims=True)
        normed = (moved * lax.rsqrt(spread + 1e-05) * gain_ref[...]).astype(jnp.bfloat16)
        for c in range(CHUNKS):
            local[c][z * held + r // step] = normed[:, c * cw : (c + 1) * cw]

    @pl.when((z > 0) & (z < last))
    def _():
        pl.semaphore_wait(barrier, dom_size + 1)

    @pl.when((z == 0) | (z == last))
    def _():
        pl.semaphore_wait(barrier, dom_size)

    def along(c, d, t):
        source = z - (t - 1) if d == 0 else z + (t - 1)
        target = z + 1 if d == 0 else z - 1
        block = local[c].at[pl.ds(source * held, held)]
        return pltpu.make_async_remote_copy(
            src_ref=block,
            dst_ref=block,
            send_sem=zsend.at[d, t - 1, c],
            recv_sem=zrecv.at[d, t - 1, c],
            device_id=(target, me),
            device_id_type=MESH,
        )

    def arriving(c, d, t):
        source = z - t if d == 0 else z + t
        block = local[c].at[pl.ds(source * held, held)]
        return pltpu.make_async_remote_copy(
            src_ref=block,
            dst_ref=block,
            send_sem=zsend.at[d, t - 1, c],
            recv_sem=zrecv.at[d, t - 1, c],
            device_id=(z - 1 if d == 0 else z + 1, me),
            device_id_type=MESH,
        )

    def sends(d, t):
        return (z >= t - 1) & (z < last) if d == 0 else (z <= last - (t - 1)) & (z > 0)

    def gets(d, t):
        return z >= t if d == 0 else z <= last - t

    def begin(c):
        for d in range(2):

            @pl.when(sends(d, 1))
            def _():
                along(c, d, 1).start()

    def across(c, o):
        target = lax.rem(me + o, dom_size)
        return pltpu.make_async_remote_copy(
            src_ref=stage.at[c, o - 1],
            dst_ref=remote.at[c, pl.ds(me * CAP, CAP)],
            send_sem=dsend.at[c, o - 1],
            recv_sem=drecv.at[c, o - 1],
            device_id=(z, target),
            device_id_type=MESH,
        )

    begin(0)
    if CHUNKS > 1:
        begin(1)
    for c in range(CHUNKS):
        for k in range(CAP):
            remote[c, me * CAP + k] = jnp.zeros((BLK, cw), jnp.bfloat16)
    for c in range(CHUNKS):
        for t in range(1, seq_size):
            for d in range(2):

                @pl.when(gets(d, t))
                def _():
                    arriving(c, d, t).wait_recv()

                if t < last:

                    @pl.when(sends(d, t + 1))
                    def _():
                        along(c, d, t + 1).start()

        if c + 2 < CHUNKS:
            begin(c + 2)
        for o in range(1, dom_size):
            target = lax.rem(me + o, dom_size)
            for k in range(CAP):
                block = pick_ref[target * CAP + k]
                stage[c, o - 1, k] = local[c][block]
            across(c, o).start()
    for c in range(CHUNKS):
        for o in range(1, dom_size):
            source = lax.rem(me + dom_size - o, dom_size)
            pltpu.make_async_remote_copy(
                src_ref=stage.at[c, o - 1],
                dst_ref=remote.at[c, pl.ds(source * CAP, CAP)],
                send_sem=dsend.at[c, o - 1],
                recv_sem=drecv.at[c, o - 1],
                device_id=(z, source),
                device_id_type=MESH,
            ).wait_recv()
            across(c, o).wait_send()
        for t in range(1, seq_size):
            for d in range(2):

                @pl.when(sends(d, t))
                def _():
                    along(c, d, t).wait_send()


def gather_rows(seq_size, dom_size, picks, node_rows, norm_gain):
    rows, width = node_rows.shape
    cw = width // CHUNKS
    vmem = pl.BlockSpec(memory_space=pltpu.VMEM)
    out = [jax.ShapeDtypeStruct((rows * seq_size // BLK, BLK, cw), jnp.bfloat16)] * CHUNKS
    out.append(jax.ShapeDtypeStruct((CHUNKS, dom_size * CAP, BLK, cw), jnp.bfloat16))
    return pl.pallas_call(
        functools.partial(gather_kernel, seq_size, dom_size),
        out_shape=out,
        in_specs=[pl.BlockSpec(memory_space=pltpu.SMEM), vmem, vmem],
        out_specs=[vmem] * (CHUNKS + 1),
        scratch_shapes=[
            pltpu.VMEM((CHUNKS, dom_size - 1, CAP, BLK, cw), jnp.bfloat16),
            pltpu.SemaphoreType.DMA((2, seq_size - 1, CHUNKS)),
            pltpu.SemaphoreType.DMA((2, seq_size - 1, CHUNKS)),
            pltpu.SemaphoreType.DMA((CHUNKS, dom_size - 1)),
            pltpu.SemaphoreType.DMA((CHUNKS, dom_size - 1)),
        ],
        compiler_params=pltpu.CompilerParams(
            collective_id=0, has_side_effects=True, vmem_limit_bytes=56 * 2**20
        ),
        name="gather_rows",
    )(picks, node_rows, norm_gain)


def attend_kernel(table_ref, meta_ref, *refs):
    local = refs[:CHUNKS]
    remote, w_ref, wo_ref, gain_ref, out_ref, k_ref, vt_ref, s_ref, mapped_ref = refs[CHUNKS:]
    g = pl.program_id(0)
    rows = out_ref.shape[0]
    local_blocks = local[0].shape[0]
    remote_blocks = remote.shape[1]
    wk = w_ref[1]
    wvt = w_ref[2].T

    def keep(x, base):
        n = x.shape[0]
        k_ref[pl.ds(pl.multiple_of(base * BLK, BLK), n), :] = dot(x, wk).astype(jnp.bfloat16)
        vt = dot(wvt, x, ((1,), (1,))).astype(jnp.bfloat16)
        for i in range(n // BLK):
            vt_ref[base + i] = vt[:, i * BLK : (i + 1) * BLK]

    def project(refs, base, count):
        step = max(n for n in range(1, 9) if count % n == 0)

        @pl.loop(0, count // step)
        def _(i):
            at = pl.ds(i * step, step)
            x = jnp.concatenate([c[at].reshape(step * BLK, -1) for c in refs], axis=1)
            keep(x, base + i * step)

    project(local, 0, local_blocks)
    project([remote.at[c] for c in range(CHUNKS)], local_blocks, remote_blocks)

    mine = pl.ds(meta_ref[0], rows // BLK)
    queries = dot(jnp.concatenate([c[mine].reshape(rows, -1) for c in local], axis=1), w_ref[0])
    queries = queries.astype(jnp.bfloat16) * jnp.bfloat16(HD**-0.5)

    head_of = lax.broadcasted_iota(jnp.int32, (GW, BLK), 0) // HD
    def score(b):
        qt = queries[b * BLK : (b + 1) * BLK, :].astype(jnp.float32).T
        spread = jnp.concatenate(
            [jnp.where(head_of == h, qt, 0.0) for h in range(GH)], axis=1
        ).astype(jnp.bfloat16)
        peak = None
        for j in range(KMAX):
            entry = table_ref[b * KMAX + j]
            keys = k_ref[pl.ds(pl.multiple_of(entry * BLK, BLK), BLK), :]
            scores = dot(keys, spread)
            if j >= KMAX - 4:
                scores = jnp.where(j < meta_ref[1 + b], scores, -jnp.inf)
            s_ref[b % 2, j] = scores
            top = jnp.max(scores.reshape(BLK // 8, 8, GH * BLK), axis=0)
            peak = top if peak is None else jnp.maximum(peak, top)
        return jnp.max(peak, axis=0, keepdims=True)

    def blend(b, peak):
        total = jnp.zeros((8, GH * BLK), jnp.float32)
        mix = jnp.zeros((GW, GH * BLK), jnp.float32)
        for j in range(0, KMAX, 2):
            parts = [jnp.exp(s_ref[b % 2, j + i] - peak) for i in range(2)]
            total += jnp.sum((parts[0] + parts[1]).reshape(BLK // 8, 8, GH * BLK), axis=0)
            weights = jnp.concatenate([p.astype(jnp.bfloat16) for p in parts], axis=0)
            values = jnp.concatenate([vt_ref[table_ref[b * KMAX + j + i]] for i in range(2)], axis=1)
            mix += dot(values, weights)
        scale = 1.0 / jnp.sum(total, axis=0, keepdims=True)
        attended = jnp.concatenate(
            [
                mix[h * HD : (h + 1) * HD, h * BLK : (h + 1) * BLK] * scale[:, h * BLK : (h + 1) * BLK]
                for h in range(GH)
            ],
            axis=0,
        )
        term = dot(attended.T.astype(jnp.bfloat16), wo_ref[...])
        at = slice(b * BLK, (b + 1) * BLK)
        mapped_ref[at, :] = jnp.where(g == 0, 0.0, mapped_ref[at, :]) + term

    query_blocks = rows // BLK
    peak = score(0)
    for b in range(query_blocks):
        later = score(b + 1) if b + 1 < query_blocks else None
        blend(b, peak)
        peak = later

    @pl.when(g == pl.num_programs(0) - 1)
    def _():
        mapped = mapped_ref[...]
        spread = jnp.mean(jnp.square(mapped), axis=-1, keepdims=True)
        out_ref[...] = (mapped * lax.rsqrt(spread + 1e-05) * gain_ref[...]).astype(jnp.bfloat16)


def attend_rows(table, meta, local, remote, weights, output_proj, final_gain, rows):
    width = output_proj.shape[0]
    blocks = local[0].shape[0] + remote.shape[1]
    vmem = pl.BlockSpec(memory_space=pltpu.VMEM)
    return pl.pallas_call(
        attend_kernel,
        out_shape=jax.ShapeDtypeStruct((rows, width), jnp.bfloat16),
        grid_spec=pltpu.PrefetchScalarGridSpec(
            num_scalar_prefetch=2,
            grid=(width // GW,),
            in_specs=[vmem] * (CHUNKS + 1)
            + [
                pl.BlockSpec((3, width, GW), lambda g, *_: (0, 0, g)),
                pl.BlockSpec((GW, width), lambda g, *_: (g, 0)),
                vmem,
            ],
            out_specs=pl.BlockSpec((rows, width), lambda g, *_: (0, 0)),
            scratch_shapes=[
                pltpu.VMEM((blocks * BLK, GW), jnp.bfloat16),
                pltpu.VMEM((blocks, GW, BLK), jnp.bfloat16),
                pltpu.VMEM((2, KMAX, BLK, GH * BLK), jnp.float32),
                pltpu.VMEM((rows, width), jnp.float32),
            ],
        ),
        compiler_params=pltpu.CompilerParams(vmem_limit_bytes=60 * 2**20),
        name="attend_rows",
    )(table, meta, *local, remote, weights, output_proj, final_gain)


def plan_lists(block_list, block_count, blocks_here, query_blocks):
    dom_size = lax.axis_size("dom")
    me = lax.axis_index("dom")
    z = lax.axis_index("seq")
    live = jnp.arange(KMAX)[None, :] < block_count[:, None]
    listed = jnp.where(live, block_list, -1).reshape(dom_size, blocks_here * KMAX)
    mine = me * blocks_here + jnp.arange(blocks_here)
    asked = jnp.any(listed[:, :, None] == mine[None, None, :], axis=1)
    before = jnp.arange(blocks_here)[:, None] < jnp.arange(blocks_here)[None, :]
    rank = jnp.sum(asked[:, :, None] & before[None], axis=1, dtype=jnp.int32)
    hit = asked[:, None, :] & (rank[:, None, :] == jnp.arange(CAP)[None, :, None])
    picks = jnp.sum(jnp.where(hit, jnp.arange(blocks_here)[None, None, :], 0), axis=2)
    every = jnp.arange(dom_size * blocks_here)
    ours = lax.dynamic_slice_in_dim(listed, me, 1, 0).reshape(-1)
    wanted = jnp.any(ours[:, None] == every[None, :], axis=0)
    entries = lax.dynamic_slice_in_dim(ours, z * query_blocks * KMAX, query_blocks * KMAX)
    safe = jnp.where(entries >= 0, entries, me * blocks_here)
    source = safe // blocks_here
    lower = (every[None, :] < safe[:, None]) & (every[None, :] >= (source * blocks_here)[:, None])
    slot = jnp.sum(lower & wanted[None, :], axis=1, dtype=jnp.int32)
    table = jnp.where(source == me, safe - me * blocks_here, blocks_here + source * CAP + slot)
    counts = lax.dynamic_slice_in_dim(block_count, me * blocks_here + z * query_blocks, query_blocks)
    meta = jnp.concatenate([jnp.reshape(z * query_blocks, (1,)), counts])
    return picks.reshape(-1), table.astype(jnp.int32), meta.astype(jnp.int32)


def on_device(nodes, norm_gain, input_proj, output_proj, final_gain, block_list, block_count):
    node_rows = nodes[0]
    rows = node_rows.shape[0]
    seq_size = lax.axis_size("seq")
    dom_size = lax.axis_size("dom")
    blocks_here = rows * seq_size // BLK
    picks, table, meta = plan_lists(block_list, block_count, blocks_here, rows // BLK)
    *local, remote = gather_rows(seq_size, dom_size, picks, node_rows, norm_gain[None, :])
    out = attend_rows(
        table, meta, local, remote, jnp.transpose(input_proj, (1, 0, 2)), output_proj,
        final_gain[None, :], rows,
    )
    return out[None]


def solution(mesh):
    placed = (P("dom", "seq", None), P(), P(), P(), P(), P(), P())
    return jax.shard_map(
        on_device, mesh=mesh, in_specs=placed, out_specs=P("dom", "seq", None), check_vma=False
    )
```

profile of v0, /device:TPU:0, one launch (start us, length us, event | category | flops | bytes accessed | tf_op | source)
XLA Modules:
  0.0 126.1 jit_solution(2948231797535123710)
XLA Ops:
  0.0 0.7 dynamic_slice.14
  0.7 0.6 pad_add_fusion.meta_ref
  1.3 0.7 fusion.3
  2.0 0.1 copy.9
  2.1 0.1 reshape.57
  2.2 0.1 fusion
  2.3 0.1 broadcast_multiply_fusion
  2.4 0.4 compare_reduce_fusion
  2.8 0.2 convert_reduce_fusion.1
  3.0 0.6 compare_select_fusion.1.table_ref
  3.6 0.1 copy.10
  3.7 0.1 convert_reduce_fusion
  3.8 0.1 select_reduce_fusion
  3.9 0.1 copy.11
  4.0 0.6 reshape.59.pick_ref
  4.6 77.6 %gather_rows.1 = (bf16[12,128,256]{2,1,0:T(8,128)(2,1)}, bf16[12,128,256]{2,1,0:T(8,128)(2,1)}, bf16[12,128,256]{2,1,0:T(8,128)(2,1)}, bf16[12,128,256]{2,1,0:T(8,128)(2,1)}, bf16[4,16,128,256]{3,2,1,0:T(8,128)(2,1)}) custom-call(s32[16]{0:T(128)} %reshape.59.pick_ref, bf16[384,1024]{1,0:T(8,128)(2,1)} %bitcast.11, f32[1,1024]{1,0:T(1,128)} %bitcast.12), custom_call_target="tpu_custom_call" | custom-call | tf_op jit(solution)/shard_map/gather_rows/pallas_call | solution.py:171
  82.2 43.9 %attend_rows.1 = bf16[384,1024]{1,0:T(8,128)(2,1)} custom-call(s32[36]{0:T(128)} %compare_select_fusion.1.table_ref, s32[4]{0:T(128)} %pad_add_fusion.meta_ref, bf16[12,128,256]{2,1,0:T(8,128)(2,1)} %get-tuple-element.10.refs_0_, bf16[12,128,256]{2,1,0:T(8,128)(2,1)} %get-tuple-element.11.refs_1_, bf16[12,128,256]{2,1,0:T(8,128)(2,1)} %get-tuple-element.12.refs_2_, ...), custom_call_target="tpu_custom_call" | custom-call | tf_op jit(solution)/shard_map/attend_rows/pallas_call | solution.py:280
  (3 shorter events, 0.0 us)
where the time goes:
time: 127 us; the launch traced here: 126 us
  Pallas kernels  122 us (96%)
  other arithmetic  2.88 us (2%)
  local copies, waits for them, and re-layouts  1.7 us (1%)
    pallas_call x1, Pallas kernels, gather_rows(): pl.pallas_call(functools.partial(gather_kernel, seq_size, dom_size), out_...  77.6 us
    pallas_call x1, Pallas kernels, attend_rows(): pl.pallas_call(attend_kernel, out_shape=jax.ShapeDtypeStruct((rows, width...  43.9 us

commit v1 on v0

--- a/solution.py
+++ b/solution.py
@@ -1,4 +1,5 @@
 import functools
+import math
 
 import jax
 import jax.numpy as jnp
@@ -11,6 +12,7 @@
 BLK = 128
 KMAX = 12
 CAP = 2
+NEAR = 4
 GW = 256
 GH = GW // HD
 CHUNKS = 4
@@ -328,17 +330,424 @@
     return picks.reshape(-1), table.astype(jnp.int32), meta.astype(jnp.int32)
 
 
+AHEAD = 2
+UNIT = 16
+SPLIT = 64
+FAR = 2**30
+
+
+def fused_kernel(
+    seq_size, dom_size, lists_ref, entries_ref, counts_ref, nodes_ref, gain_ref, final_ref, w_hbm, wo_hbm,
+    out_ref, x_ref, snap_ref, stage_ref, w_ref, kv_ref, q_ref, s_ref, peak_ref, sum_ref, near_ref,
+    att_ref, pick_ref, first_ref, table_ref, zsend, zrecv, dsend, drecv, wsem,
+):
+    rows, width = nodes_ref.shape
+    held = rows // BLK
+    local_blocks = held * seq_size
+    far_blocks = dom_size * CAP
+    units = BLK // UNIT
+    groups = width // GW
+    heads = GH * BLK
+    z = lax.axis_index("seq")
+    me = lax.axis_index("dom")
+    last = seq_size - 1
+
+    barrier = pltpu.get_barrier_semaphore()
+
+    @pl.when(z > 0)
+    def _():
+        pl.semaphore_signal(barrier, inc=1, device_id=(z - 1, me), device_id_type=MESH)
+
+    @pl.when(z < last)
+    def _():
+        pl.semaphore_signal(barrier, inc=1, device_id=(z + 1, me), device_id_type=MESH)
+
+    for o in range(1, dom_size):
+        pl.semaphore_signal(
+            barrier, inc=1, device_id=(z, lax.rem(me + o, dom_size)), device_id_type=MESH
+        )
+
+    loads = [pltpu.make_async_copy(w_hbm.at[i], w_ref.at[i], wsem.at[i]) for i in range(3)]
+    load_out = pltpu.make_async_copy(wo_hbm, w_ref.at[0], wsem.at[3])
+    for load in loads:
+        load.start()
+
+    for r in range(held):
+        wide = nodes_ref[r * BLK : (r + 1) * BLK, :].astype(jnp.float32)
+        center = jnp.mean(wide, axis=-1, keepdims=True)
+        moved = wide - center
+        spread = jnp.mean(jnp.square(moved), axis=-1, keepdims=True)
+        normed = (moved * lax.rsqrt(spread + 1e-05) * gain_ref[...]).astype(jnp.bfloat16)
+        for u in range(units):
+            x_ref[u, z * held + r] = normed[u * UNIT : (u + 1) * UNIT, :]
+
+    @pl.when((z > 0) & (z < last))
+    def _():
+        pl.semaphore_wait(barrier, dom_size + 1)
+
+    @pl.when((z == 0) | (z == last))
+    def _():
+        pl.semaphore_wait(barrier, dom_size)
+
+    def hop(u, d, t, source, target):
+        block = x_ref.at[u, pl.ds(source * held, held)]
+        return pltpu.make_async_remote_copy(
+            src_ref=block,
+            dst_ref=block,
+            send_sem=zsend.at[d, t - 1, u],
+            recv_sem=zrecv.at[d, t - 1, u],
+            device_id=(target, me),
+            device_id_type=MESH,
+        )
+
+    def along(u, d, t):
+        return hop(u, d, t, z - (t - 1) if d == 0 else z + (t - 1), z + 1 if d == 0 else z - 1)
+
+    def arriving(u, d, t):
+        return hop(u, d, t, z - t if d == 0 else z + t, z - 1 if d == 0 else z + 1)
+
+    def sends(d, t):
+        return (z >= t - 1) & (z < last) if d == 0 else (z <= last - (t - 1)) & (z > 0)
+
+    def gets(d, t):
+        return z >= t if d == 0 else z <= last - t
+
+    def begin(u, inner):
+        for d in range(2):
+            edge = 0 if d == 0 else last
+
+            @pl.when(sends(d, 1) & ((z != edge) if inner else (z == edge)))
+            def _():
+                along(u, d, 1).start()
+
+    def picked(u, o, source, partner):
+        return pltpu.make_async_remote_copy(
+            src_ref=stage_ref.at[u, o - 1],
+            dst_ref=x_ref.at[u, pl.ds(local_blocks + source * CAP, CAP)],
+            send_sem=dsend.at[u, o - 1],
+            recv_sem=drecv.at[u, o - 1],
+            device_id=(z, partner),
+            device_id_type=MESH,
+        )
+
+    def across(u, o):
+        return picked(u, o, me, lax.rem(me + o, dom_size))
+
+    def take(u):
+        for o in range(1, dom_size):
+            source = lax.rem(me + dom_size - o, dom_size)
+            picked(u, o, source, source).wait_recv()
+
+    for u in range(units):
+        begin(u, False)
+        if u < AHEAD:
+            begin(u, True)
+
+    lists = lists_ref[...]
+    lane = lax.broadcasted_iota(jnp.int32, lists.shape, 1)
+    mine = (lists >= me * local_blocks) & (lists < (me + 1) * local_blocks)
+    for o in range(1, dom_size):
+        target = lax.rem(me + o, dom_size)
+        theirs = (lane >= target * local_blocks) & (lane < (target + 1) * local_blocks)
+        low = jnp.min(jnp.where(mine & theirs, lists, FAR))
+        high = jnp.max(jnp.where(mine & theirs, lists, -1))
+        pick_ref[(o - 1) * CAP] = jnp.where(low < FAR, low - me * local_blocks, 0)
+        pick_ref[(o - 1) * CAP + 1] = jnp.where(high >= 0, high - me * local_blocks, 0)
+    ours = (lane >= me * local_blocks) & (lane < (me + 1) * local_blocks)
+    for s in range(dom_size):
+        inside = (lists >= s * local_blocks) & (lists < (s + 1) * local_blocks)
+        first_ref[s] = jnp.min(jnp.where(ours & inside, lists, FAR))
+    at = me * local_blocks + z * held
+    for b in range(held):
+        for j in range(KMAX):
+            entry = entries_ref[j, at + b]
+            slot = z * held + b
+            if j < NEAR:
+                inside = (entry >= me * local_blocks) & (entry < (me + 1) * local_blocks)
+                table_ref[b * KMAX + j] = jnp.where(inside, entry - me * local_blocks, slot)
+            else:
+                for s in range(dom_size):
+                    place = local_blocks + s * CAP + jnp.where(entry == first_ref[s], 0, 1)
+                    inside = (entry >= s * local_blocks) & (entry < (s + 1) * local_blocks)
+                    slot = jnp.where(inside, place, slot)
+                table_ref[b * KMAX + j] = slot
+
+    for u in range(units):
+        for k in range(CAP):
+            x_ref[u, local_blocks + me * CAP + k] = jnp.zeros((UNIT, width), jnp.bfloat16)
+
+    def project(kv, first, count, u, n):
+        blocks = slice(first, first + count)
+        x = x_ref[pl.ds(u, n), blocks].reshape(n * count * UNIT, width)
+        for g in range(groups):
+            cols = slice(g * GW, (g + 1) * GW)
+            made = dot(x, w_ref[1 + kv, :, cols]).astype(jnp.bfloat16).reshape(n, count, UNIT, GW)
+            for i in range(n):
+                at_rows = pl.ds(pl.multiple_of((u + i) * UNIT, UNIT), UNIT)
+                kv_ref[kv, blocks, at_rows, cols] = made[i]
+
+    def project_queries():
+        for load in loads:
+            load.wait()
+        x = x_ref[:, pl.ds(z * held, held)].reshape(rows, width)
+        for g in range(groups):
+            cols = slice(g * GW, (g + 1) * GW)
+            made = dot(x, w_ref[0, :, cols]).astype(jnp.bfloat16) * jnp.bfloat16(HD**-0.5)
+            q_ref[:, :, :, cols] = made.reshape(units, held, UNIT, GW)
+        load_out.start()
+
+    head_of = lax.broadcasted_iota(jnp.int32, (BLK, GW), 1) // HD
+
+    def attend(b, start, end):
+        span = end - start
+        tiles = KMAX * span // BLK
+        each = BLK // span
+        nth = lax.broadcasted_iota(jnp.int32, (1, BLK), 1) // span
+
+        def gathered(kv, g, tile, n):
+            entries = range(tile * each, (tile + n) * each)
+            return jnp.concatenate(
+                [kv_ref[kv, table_ref[b * KMAX + j], start:end, g * GW : (g + 1) * GW] for j in entries],
+                axis=0,
+            )
+
+        def spans():
+            return [(i, min(2, tiles - i)) for i in range(0, tiles, 2)]
+
+        def score(g):
+            q = q_ref[:, b, :, g * GW : (g + 1) * GW].reshape(BLK, GW)
+            wide = jnp.concatenate([jnp.where(head_of == h, q, jnp.bfloat16(0)) for h in range(GH)], axis=0)
+            peak = None
+            for tile, n in spans():
+                both = dot(wide, gathered(0, g, tile, n), ((1,), (1,)))
+                for i in range(n):
+                    scores = both[:, i * BLK : (i + 1) * BLK]
+                    if (tile + i + 1) * each > KMAX - 4:
+                        live = nth + (tile + i) * each < counts_ref[at + b]
+                        scores = jnp.where(live, scores, -jnp.inf)
+                    s_ref[(g % 2) * MOST + tile + i] = scores
+                    peak = scores if peak is None else jnp.maximum(peak, scores)
+            peak = jnp.broadcast_to(jnp.max(peak, axis=1, keepdims=True), (heads, BLK))
+            return peak if start == 0 else jnp.maximum(peak, peak_ref[b * groups + g])
+
+        def blend(g, peak):
+            total = jnp.zeros((heads, BLK), jnp.float32)
+            mix = jnp.zeros((heads, GW), jnp.float32)
+            for tile, n in spans():
+                parts = [jnp.exp(s_ref[(g % 2) * MOST + tile + i] - peak) for i in range(n)]
+                for part in parts:
+                    total += part
+                weights = jnp.concatenate([part.astype(jnp.bfloat16) for part in parts], axis=1)
+                mix += dot(weights, gathered(1, g, tile, n))
+            return jnp.broadcast_to(jnp.sum(total, axis=1, keepdims=True), (heads, BLK)), mix
+
+        def own_heads(part_of):
+            kept = None
+            for h in range(GH):
+                part = jnp.where(head_of == h, part_of(h), 0.0)
+                kept = part if kept is None else kept + part
+            return kept
+
+        def rows_of(x, h):
+            return x[h * BLK : (h + 1) * BLK]
+
+        def over(x, h):
+            return jnp.concatenate([rows_of(x, h)] * (GW // BLK), axis=1)
+
+        peak = score(0)
+        for g in range(groups):
+            n = b * groups + g
+            later = score(g + 1) if g + 1 < groups else None
+            total, mix = blend(g, peak)
+            if start == 0:
+                kept = own_heads(lambda h: rows_of(mix, h))
+            else:
+                fade = jnp.exp(peak_ref[n] - peak)
+                total = total + sum_ref[n] * fade
+                near = near_ref[n]
+                if end == BLK:
+                    scale = 1.0 / total
+                    fade = fade * scale
+                    kept = own_heads(lambda h: rows_of(mix, h) * over(scale, h) + near * over(fade, h))
+                else:
+                    kept = own_heads(lambda h: rows_of(mix, h) + near * over(fade, h))
+            if end == BLK:
+                at_rows = pl.ds(pl.multiple_of(b * BLK, BLK), BLK)
+                att_ref[at_rows, g * GW : (g + 1) * GW] = kept.astype(jnp.bfloat16)
+            else:
+                peak_ref[n] = peak
+                sum_ref[n] = total
+                near_ref[n] = kept
+            peak = later
+
+    @pl.loop(0, units)
+    def _(u):
+        odd = lax.rem(u, 2)
+        for t in range(1, seq_size):
+            for d in range(2):
+
+                @pl.when(gets(d, t))
+                def _():
+                    arriving(u, d, t).wait_recv()
+
+                if t < last:
+
+                    @pl.when(sends(d, t + 1))
+                    def _():
+                        along(u, d, t + 1).start()
+
+            if t == last:
+
+                @pl.when(u + AHEAD < units)
+                def _():
+                    begin(u + AHEAD, True)
+
+                snap_ref[...] = x_ref[u, 0:local_blocks]
+                for o in range(1, dom_size):
+                    for k in range(CAP):
+                        stage_ref[u, o - 1, k] = snap_ref[pick_ref[(o - 1) * CAP + k]]
+                    across(u, o).start()
+
+                @pl.when(u == 0)
+                def _():
+                    project_queries()
+
+            for kv in range(2):
+                if t == min(kv + 1, last):
+
+                    @pl.when((u >= 2) & (odd == 0))
+                    def _():
+                        project(kv, 0, local_blocks, u - 2, 2)
+
+                    @pl.when((u >= 3) & (odd == 1))
+                    def _():
+                        if kv == 0:
+                            take(u - 3)
+                            take(u - 2)
+                        project(kv, local_blocks, far_blocks, u - 3, 2)
+
+            if t == last:
+
+                @pl.when(u >= units - 2)
+                def _():
+                    late = u - (units - 2)
+                    most = held - held // 2
+
+                    @pl.loop(late * most, most + late * (held - most))
+                    def _(b):
+                        attend(b, 0, SPLIT)
+
+    for kv in range(2):
+        project(kv, 0, local_blocks, units - 2, 2)
+
+    @pl.loop(units - 2, units)
+    def _(u):
+        take(u)
+        for kv in range(2):
+            project(kv, local_blocks, far_blocks, u, 1)
+
+    @pl.loop(0, held)
+    def _(b):
+        attend(b, SPLIT, BLK)
+
+    load_out.wait()
+    part = GW // BLK
+    squares = jnp.zeros((rows, BLK), jnp.float32)
+    for g in range(groups):
+        mapped = dot(att_ref[...], w_ref[0, :, g * GW : (g + 1) * GW])
+        for i in range(part):
+            piece_of = mapped[:, i * BLK : (i + 1) * BLK]
+            s_ref[g * part + i, 0:rows, :] = piece_of
+            squares += jnp.square(piece_of)
+    norm = lax.rsqrt(jnp.sum(squares, axis=1, keepdims=True) * (1.0 / width) + 1e-05)
+    for i in range(groups * part):
+        cols = slice(i * BLK, (i + 1) * BLK)
+        out_ref[:, cols] = (s_ref[i, 0:rows, :] * norm * final_ref[:, cols]).astype(jnp.bfloat16)
+
+    @pl.loop(0, units)
+    def _(u):
+        for o in range(1, dom_size):
+            across(u, o).wait_send()
+        for t in range(1, seq_size):
+            for d in range(2):
+
+                @pl.when(sends(d, t))
+                def _():
+                    along(u, d, t).wait_send()
+
+
+MOST = KMAX * max(SPLIT, BLK - SPLIT) // BLK
+
+
+def fused_scratch(seq_size, dom_size, rows, width):
+    units = BLK // UNIT
+    held = rows // BLK
+    local_blocks = held * seq_size
+    blocks = local_blocks + dom_size * CAP
+    steps = held * (width // GW)
+    heads = GH * BLK
+    f32, bf16, i32 = jnp.float32, jnp.bfloat16, jnp.int32
+    arrays = [
+        ((units, blocks, UNIT, width), bf16),
+        ((local_blocks, UNIT, width), bf16),
+        ((units, dom_size - 1, CAP, UNIT, width), bf16),
+        ((3, width, width), bf16),
+        ((2, blocks, BLK, width), bf16),
+        ((units, held, UNIT, width), bf16),
+        ((2 * MOST, heads, BLK), f32),
+        ((steps, heads, BLK), f32),
+        ((steps, heads, BLK), f32),
+        ((steps, BLK, GW), f32),
+        ((rows, width), bf16),
+    ]
+    size = sum(math.prod(shape) * jnp.dtype(kind).itemsize for shape, kind in arrays)
+    scratch = [pltpu.VMEM(shape, kind) for shape, kind in arrays]
+    scratch += [pltpu.SMEM((n,), i32) for n in (CAP * (dom_size - 1), dom_size, held * KMAX)]
+    scratch += [
+        pltpu.SemaphoreType.DMA((2, seq_size - 1, units)),
+        pltpu.SemaphoreType.DMA((2, seq_size - 1, units)),
+        pltpu.SemaphoreType.DMA((units, dom_size - 1)),
+        pltpu.SemaphoreType.DMA((units, dom_size - 1)),
+        pltpu.SemaphoreType.DMA((4,)),
+    ]
+    return scratch, width <= BLK * 2 * MOST and rows <= heads and size < 50 * 2**20
+
+
+def fused_layer(seq_size, dom_size, scratch, node_rows, norm_gain, weights, output_proj, final_gain, lists, counts):
+    vmem = pl.BlockSpec(memory_space=pltpu.VMEM)
+    smem = pl.BlockSpec(memory_space=pltpu.SMEM)
+    hbm = pl.BlockSpec(memory_space=pl.ANY)
+    return pl.pallas_call(
+        functools.partial(fused_kernel, seq_size, dom_size),
+        out_shape=jax.ShapeDtypeStruct(node_rows.shape, jnp.bfloat16),
+        in_specs=[vmem, smem, smem, vmem, vmem, vmem, hbm, hbm],
+        out_specs=vmem,
+        scratch_shapes=scratch,
+        compiler_params=pltpu.CompilerParams(
+            collective_id=1, has_side_effects=True, vmem_limit_bytes=60 * 2**20
+        ),
+        name="fused_layer",
+    )(lists, lists, counts, node_rows, norm_gain, final_gain, weights, output_proj)
+
+
 def on_device(nodes, norm_gain, input_proj, output_proj, final_gain, block_list, block_count):
     node_rows = nodes[0]
     rows = node_rows.shape[0]
     seq_size = lax.axis_size("seq")
     dom_size = lax.axis_size("dom")
+    weights = jnp.transpose(input_proj, (1, 0, 2))
+    scratch, fits = fused_scratch(seq_size, dom_size, rows, node_rows.shape[1])
+    if fits:
+        out = fused_layer(
+            seq_size, dom_size, scratch, node_rows, norm_gain[None, :], weights, output_proj,
+            final_gain[None, :], block_list.T, block_count,
+        )
+        return out[None]
     blocks_here = rows * seq_size // BLK
     picks, table, meta = plan_lists(block_list, block_count, blocks_here, rows // BLK)
     *local, remote = gather_rows(seq_size, dom_size, picks, node_rows, norm_gain[None, :])
     out = attend_rows(
-        table, meta, local, remote, jnp.transpose(input_proj, (1, 0, 2)), output_proj,
-        final_gain[None, :], rows,
+        table, meta, local, remote, weights, output_proj, final_gain[None, :], rows,
     )
     return out[None]
 

time: 127 us -> 84.7 us (0.67)
  Pallas kernels: 122 us -> 82.4 us
  other arithmetic: 2.88 us -> 0 us
    pallas_call x2 -> x1, Pallas kernels: 122 us -> 82.4 us  [fused_layer(): pl.pallas_call(functools.partial(fused_kernel, seq_size, dom_size), out_s...]
    unnamed x0 -> x1, local copies, waits for them, and re-layouts: none -> 2.06 us
    select_n x2 -> x0, other arithmetic: 1.31 us -> none  [the longest x1 0.71 us: plan_lists(): jnp.where(live, block_list, -1).reshape(dom_size, blocks_here * KMAX)]
where the time goes in v1:
time: 84.7 us; the launch traced here: 84.5 us
  Pallas kernels  82.4 us (97%)
  local copies, waits for them, and re-layouts  2.06 us (2%)
    pallas_call x1, Pallas kernels, fused_layer(): pl.pallas_call(functools.partial(fused_kernel, seq_size, dom_size), out_s...  82.4 us
    unnamed x1, local copies, waits for them, and re-layouts  2.06 us

profile of v1, /device:TPU:0, one launch (start us, length us, event | category | flops | bytes accessed | tf_op | source)
XLA Modules:
  0.0 84.5 jit_solution(1430398466938501314)
XLA Ops:
  0.0 82.4 %fused_layer.1 = bf16[384,1024]{1,0:T(8,128)(2,1)} custom-call(s32[12,96]{1,0:T(8,128)} %bitcast.9, s32[12,96]{1,0:T(8,128)} %bitcast.10, s32[96]{0:T(128)} %counts_ref.1, bf16[384,1024]{1,0:T(8,128)(2,1)} %bitcast.8, f32[1,1024]{1,0:T(1,128)} %bitcast.11, f32[1,1024]{1,0:T(1,128)} %bitcast.12, bf16[3,1024,1024]{2,1,0:T(8,128)(2,1)} %bitcast.6, ...), custom_call_target="tpu_custom_call" | custom-call | tf_op jit(solution)/shard_map/fused_layer/pallas_call | solution.py:720
  82.4 2.1 %copy.9 = bf16[1,384,1024]{2,1,0:T(8,128)(2,1)} copy(bf16[1,384,1024]{2,1,0:T(8,128)(2,1)} %bitcast.7) | data formatting | bytes 1572864

commit v2 on v1

--- a/solution.py
+++ b/solution.py
@@ -337,8 +337,8 @@
 
 
 def fused_kernel(
-    seq_size, dom_size, lists_ref, entries_ref, counts_ref, nodes_ref, gain_ref, final_ref, w_hbm, wo_hbm,
-    out_ref, x_ref, snap_ref, stage_ref, w_ref, kv_ref, q_ref, s_ref, peak_ref, sum_ref, near_ref,
+    seq_size, dom_size, lists_ref, entries_ref, counts_ref, gain_ref, final_ref, nodes_hbm, w_hbm, wo_hbm,
+    out_ref, nodes_ref, x_ref, snap_ref, stage_ref, w_ref, kv_ref, q_ref, s_ref, peak_ref, sum_ref, near_ref,
     att_ref, pick_ref, first_ref, table_ref, zsend, zrecv, dsend, drecv, wsem,
 ):
     rows, width = nodes_ref.shape
@@ -367,19 +367,25 @@
             barrier, inc=1, device_id=(z, lax.rem(me + o, dom_size)), device_id_type=MESH
         )
 
+    load_nodes = pltpu.make_async_copy(nodes_hbm, nodes_ref, wsem.at[4])
+    load_nodes.start()
     loads = [pltpu.make_async_copy(w_hbm.at[i], w_ref.at[i], wsem.at[i]) for i in range(3)]
     load_out = pltpu.make_async_copy(wo_hbm, w_ref.at[0], wsem.at[3])
     for load in loads:
         load.start()
 
-    for r in range(held):
-        wide = nodes_ref[r * BLK : (r + 1) * BLK, :].astype(jnp.float32)
-        center = jnp.mean(wide, axis=-1, keepdims=True)
-        moved = wide - center
-        spread = jnp.mean(jnp.square(moved), axis=-1, keepdims=True)
-        normed = (moved * lax.rsqrt(spread + 1e-05) * gain_ref[...]).astype(jnp.bfloat16)
-        for u in range(units):
-            x_ref[u, z * held + r] = normed[u * UNIT : (u + 1) * UNIT, :]
+    def normalize(first, end):
+        for r in range(held):
+            wide = nodes_ref[r * BLK + first * UNIT : r * BLK + end * UNIT, :].astype(jnp.float32)
+            center = jnp.mean(wide, axis=-1, keepdims=True)
+            moved = wide - center
+            spread = jnp.mean(jnp.square(moved), axis=-1, keepdims=True)
+            normed = (moved * lax.rsqrt(spread + 1e-05) * gain_ref[...]).astype(jnp.bfloat16)
+            for u in range(first, end):
+                x_ref[u, z * held + r] = normed[(u - first) * UNIT : (u - first + 1) * UNIT, :]
+
+    load_nodes.wait()
+    normalize(0, AHEAD)
 
     @pl.when((z > 0) & (z < last))
     def _():
@@ -438,10 +444,12 @@
             source = lax.rem(me + dom_size - o, dom_size)
             picked(u, o, source, source).wait_recv()
 
-    for u in range(units):
+    for u in range(AHEAD):
         begin(u, False)
-        if u < AHEAD:
-            begin(u, True)
+        begin(u, True)
+    normalize(AHEAD, units)
+    for u in range(AHEAD, units):
+        begin(u, False)
 
     lists = lists_ref[...]
     lane = lax.broadcasted_iota(jnp.int32, lists.shape, 1)
@@ -542,10 +550,9 @@
             return jnp.broadcast_to(jnp.sum(total, axis=1, keepdims=True), (heads, BLK)), mix
 
         def own_heads(part_of):
-            kept = None
-            for h in range(GH):
-                part = jnp.where(head_of == h, part_of(h), 0.0)
-                kept = part if kept is None else kept + part
+            kept = part_of(GH - 1)
+            for h in range(GH - 1):
+                kept = jnp.where(head_of == h, part_of(h), kept)
             return kept
 
         def rows_of(x, h):
@@ -559,18 +566,13 @@
             n = b * groups + g
             later = score(g + 1) if g + 1 < groups else None
             total, mix = blend(g, peak)
-            if start == 0:
-                kept = own_heads(lambda h: rows_of(mix, h))
-            else:
+            kept = own_heads(lambda h: rows_of(mix, h))
+            if start > 0:
                 fade = jnp.exp(peak_ref[n] - peak)
                 total = total + sum_ref[n] * fade
-                near = near_ref[n]
-                if end == BLK:
-                    scale = 1.0 / total
-                    fade = fade * scale
-                    kept = own_heads(lambda h: rows_of(mix, h) * over(scale, h) + near * over(fade, h))
-                else:
-                    kept = own_heads(lambda h: rows_of(mix, h) + near * over(fade, h))
+                kept = kept + near_ref[n] * own_heads(lambda h: over(fade, h))
+            if end == BLK:
+                kept = kept / own_heads(lambda h: over(total, h))
             if end == BLK:
                 at_rows = pl.ds(pl.multiple_of(b * BLK, BLK), BLK)
                 att_ref[at_rows, g * GW : (g + 1) * GW] = kept.astype(jnp.bfloat16)
@@ -688,6 +690,7 @@
     heads = GH * BLK
     f32, bf16, i32 = jnp.float32, jnp.bfloat16, jnp.int32
     arrays = [
+        ((rows, width), bf16),
         ((units, blocks, UNIT, width), bf16),
         ((local_blocks, UNIT, width), bf16),
         ((units, dom_size - 1, CAP, UNIT, width), bf16),
@@ -708,9 +711,9 @@
         pltpu.SemaphoreType.DMA((2, seq_size - 1, units)),
         pltpu.SemaphoreType.DMA((units, dom_size - 1)),
         pltpu.SemaphoreType.DMA((units, dom_size - 1)),
-        pltpu.SemaphoreType.DMA((4,)),
+        pltpu.SemaphoreType.DMA((5,)),
     ]
-    return scratch, width <= BLK * 2 * MOST and rows <= heads and size < 50 * 2**20
+    return scratch, width <= BLK * 2 * MOST and rows <= heads and size < 51 * 2**20
 
 
 def fused_layer(seq_size, dom_size, scratch, node_rows, norm_gain, weights, output_proj, final_gain, lists, counts):
@@ -720,14 +723,14 @@
     return pl.pallas_call(
         functools.partial(fused_kernel, seq_size, dom_size),
         out_shape=jax.ShapeDtypeStruct(node_rows.shape, jnp.bfloat16),
-        in_specs=[vmem, smem, smem, vmem, vmem, vmem, hbm, hbm],
+        in_specs=[vmem, smem, smem, vmem, vmem, hbm, hbm, hbm],
         out_specs=vmem,
         scratch_shapes=scratch,
         compiler_params=pltpu.CompilerParams(
             collective_id=1, has_side_effects=True, vmem_limit_bytes=60 * 2**20
         ),
         name="fused_layer",
-    )(lists, lists, counts, node_rows, norm_gain, final_gain, weights, output_proj)
+    )(lists, lists, counts, norm_gain, final_gain, node_rows, weights, output_proj)
 
 
 def on_device(nodes, norm_gain, input_proj, output_proj, final_gain, block_list, block_count):

time: 84.7 us -> 84.4 us (level)
  no operation moved by 1% of the time
where the time goes in v2:
time: 84.4 us; the launch traced here: 84.2 us
  Pallas kernels  82.2 us (97%)
  local copies, waits for them, and re-layouts  2.06 us (2%)
    pallas_call x1, Pallas kernels, fused_layer(): pl.pallas_call(functools.partial(fused_kernel, seq_size, dom_size), out_s...  82.2 us
    unnamed x1, local copies, waits for them, and re-layouts  2.06 us

profile of v2, /device:TPU:0, one launch (start us, length us, event | category | flops | bytes accessed | tf_op | source)
XLA Modules:
  0.0 84.2 jit_solution(2191798381575152503)
XLA Ops:
  0.0 82.2 %fused_layer.1 = bf16[384,1024]{1,0:T(8,128)(2,1)} custom-call(s32[12,96]{1,0:T(8,128)} %bitcast.9, s32[12,96]{1,0:T(8,128)} %bitcast.10, s32[96]{0:T(128)} %counts_ref.1, f32[1,1024]{1,0:T(1,128)} %bitcast.11, f32[1,1024]{1,0:T(1,128)} %bitcast.12, bf16[384,1024]{1,0:T(8,128)(2,1)} %bitcast.8, bf16[3,1024,1024]{2,1,0:T(8,128)(2,1)} %bitcast.6, ...), custom_call_target="tpu_custom_call" | custom-call | tf_op jit(solution)/shard_map/fused_layer/pallas_call | solution.py:723
  82.2 2.1 %copy.9 = bf16[1,384,1024]{2,1,0:T(8,128)(2,1)} copy(bf16[1,384,1024]{2,1,0:T(8,128)(2,1)} %bitcast.7) | data formatting | bytes 1572864

commit v3 on v2

--- a/solution.py
+++ b/solution.py
@@ -605,7 +605,7 @@
                     begin(u + AHEAD, True)
 
                 snap_ref[...] = x_ref[u, 0:local_blocks]
-                for o in range(1, dom_size):
+                for o in sorted(range(1, dom_size), key=lambda o: abs(2 * o - dom_size)):
                     for k in range(CAP):
                         stage_ref[u, o - 1, k] = snap_ref[pick_ref[(o - 1) * CAP + k]]
                     across(u, o).start()

time: 84.4 us -> 84.4 us (level)
  no operation moved by 1% of the time
where the time goes in v3:
time: 84.4 us; the launch traced here: 84.2 us
  Pallas kernels  82.2 us (97%)
  local copies, waits for them, and re-layouts  2.06 us (2%)
    pallas_call x1, Pallas kernels, fused_layer(): pl.pallas_call(functools.partial(fused_kernel, seq_size, dom_size), out_s...  82.2 us
    unnamed x1, local copies, waits for them, and re-layouts  2.06 us

profile of v3, /device:TPU:0, one launch (start us, length us, event | category | flops | bytes accessed | tf_op | source)
XLA Modules:
  0.0 84.2 jit_solution(4976636059604529081)
XLA Ops:
  0.0 82.2 %fused_layer.1 = bf16[384,1024]{1,0:T(8,128)(2,1)} custom-call(s32[12,96]{1,0:T(8,128)} %bitcast.9, s32[12,96]{1,0:T(8,128)} %bitcast.10, s32[96]{0:T(128)} %counts_ref.1, f32[1,1024]{1,0:T(1,128)} %bitcast.11, f32[1,1024]{1,0:T(1,128)} %bitcast.12, bf16[384,1024]{1,0:T(8,128)(2,1)} %bitcast.8, bf16[3,1024,1024]{2,1,0:T(8,128)(2,1)} %bitcast.6, ...), custom_call_target="tpu_custom_call" | custom-call | tf_op jit(solution)/shard_map/fused_layer/pallas_call | solution.py:723
  82.2 2.1 %copy.9 = bf16[1,384,1024]{2,1,0:T(8,128)(2,1)} copy(bf16[1,384,1024]{2,1,0:T(8,128)(2,1)} %bitcast.7) | data formatting | bytes 1572864
